TPU v7x, 256 devices: a whole 4x4x8 slice. The times are simulated.
256 devices in a mesh: expert: 32 (over y, x, core), tensor: 8 (over z).
Axes of the slice: x: 4, y: 4, z: 8, core: 2. Of those that a mesh axis runs over, the one named last changes fastest.
Arguments:
- tokens: bfloat16 [16384, 4096], P('expert', 'tensor'), may hold values from -36 to 36
- expert_ids: int32 [16384, 1], P('expert'), may hold values from 0 to 63; in each aligned block of 512 rows (0 to 511, 512 to 1023, ...) at most 16 rows name the same one
- gates: float32 [16384, 1], P('expert'), may hold values from 0.25 to 1
- expert_in: bfloat16 [64, 4096, 2048], P('expert', 'tensor'), may hold values from -0.09375 to 0.09375
- expert_out: bfloat16 [64, 2048, 4096], P('expert', None, 'tensor'), may hold values from -0.125 to 0.125
- norm_gain: float32 [4096], replicated, may hold values from 0.5 to 2
- up_weight: bfloat16 [4096, 8192], P('expert', 'tensor'), may hold values from -0.09375 to 0.09375
- down_weight: bfloat16 [4096, 8192], P('expert', 'tensor'), may hold values from -0.0625 to 0.0625
Outputs:
- layer_output: bfloat16 [16384, 4096], P('expert', 'tensor')
Inputs may be any that keep to these rules, and one draw needn't show every extreme that they name: `expert_ids`: among the 512 tokens of one block, at most 16 carry the same expert id; in some blocks one id is carried by exactly 16 tokens.
All inputs are finite; a program needn't handle non-finite values.
Results may differ from a plain program's by a relative error of at most 0.015.
Values may be sent and summed in bfloat16 or wider, within the bound.
No kernel may reach another device: no remote copies, remote signals or barrier semaphores. Data moves between devices by JAX's collectives and lax.ppermute only.
A program may use at most 128 MiB of HBM per device.

v0:
```python
import jax
import jax.numpy as jnp
from jax import lax
from jax.sharding import PartitionSpec as P

EXP_DEV = 2


def slot_table(expert_col, experts, capacity):
    expert = expert_col[:, 0]
    onehot = (expert[:, None] == jnp.arange(experts, dtype=jnp.int32)[None, :]).astype(jnp.int32)
    before = jnp.cumsum(onehot, axis=0) - onehot
    position = jnp.sum(before * onehot, axis=1)
    slot_index = expert * capacity + position
    selector = jnp.arange(experts * capacity, dtype=jnp.int32)[:, None] == slot_index[None, :]
    return selector.astype(jnp.bfloat16)


def trade(buffer):
    result = lax.all_to_all(buffer, "expert", split_axis=0, concat_axis=0, tiled=True)
    return result


def gather_rows(weight, combine, start_value):
    return combine(start_value, lax.all_gather(weight, "expert", axis=0, tiled=True), jnp.int32(0))


def shards(tokens, expert_ids, gates, expert_in, expert_out, norm_gain, up_weight, down_weight):
    token_count = tokens.shape[0]
    local_width = tokens.shape[1]
    groups = lax.axis_size("expert")
    experts = EXP_DEV * groups
    capacity = 2 * token_count // experts
    selector = slot_table(expert_ids, experts, capacity)
    outgoing = jnp.dot(selector, tokens, preferred_element_type=jnp.float32).astype(jnp.bfloat16)
    outgoing = outgoing.reshape(groups, EXP_DEV, capacity, local_width)
    arrived = trade(outgoing)
    partial_value = jnp.einsum(
        "sjcd,jdh->sjch", arrived, expert_in, preferred_element_type=jnp.float32
    )
    summed = lax.psum(partial_value.astype(jnp.bfloat16), "tensor").astype(jnp.float32)
    active = jax.nn.relu(summed).astype(jnp.bfloat16)
    produced = jnp.einsum(
        "sjch,jhd->sjcd", active, expert_out, preferred_element_type=jnp.float32
    ).astype(jnp.bfloat16)
    returned = trade(produced).reshape(experts * capacity, local_width)
    routed = lax.dot_general(
        selector, returned, (((0,), (0,)), ((), ())), preferred_element_type=jnp.float32
    )
    mixed = (tokens.astype(jnp.float32) + gates * routed).astype(jnp.bfloat16)
    whole = lax.all_gather(mixed, "tensor", axis=1, tiled=True)
    whole_f32 = whole.astype(jnp.float32)
    mean_square = jnp.mean(whole_f32 * whole_f32, axis=1, keepdims=True)
    normed = (whole_f32 * lax.rsqrt(mean_square + 1e-06) * norm_gain).astype(jnp.bfloat16)

    def add_up(carry, piece, start):
        return jnp.dot(normed, piece, preferred_element_type=jnp.float32)

    ffn_hidden = gather_rows(
        up_weight, add_up, jnp.zeros((token_count, up_weight.shape[1]), jnp.float32)
    )
    ffn_active = jax.nn.gelu(ffn_hidden, approximate=True).astype(jnp.bfloat16)

    def add_down(carry, piece, start):
        contribution = lax.dot_general(
            ffn_active, piece, (((1,), (1,)), ((), ())), preferred_element_type=jnp.float32
        )
        return contribution

    outputs = gather_rows(
        down_weight, add_down, jnp.zeros((token_count, whole.shape[1]), jnp.float32)
    )
    summed_out = lax.psum_scatter(
        outputs.astype(jnp.bfloat16), "tensor", scatter_dimension=1, tiled=True
    ).astype(jnp.float32)
    return (mixed.astype(jnp.float32) + summed_out).astype(jnp.bfloat16)


def solution(mesh):
    return jax.shard_map(
        shards,
        mesh=mesh,
        in_specs=(
            P("expert", "tensor"),
            P("expert", None),
            P("expert", None),
            P("expert", "tensor", None),
            P("expert", None, "tensor"),
            P(),
            P("expert", "tensor"),
            P("expert", "tensor"),
        ),
        out_specs=P("expert", "tensor"),
        check_vma=False,
    )
```

profile of v0, /device:TPU:1, one launch (start us, length us, event | category | flops | bytes accessed | tf_op | source)
XLA Modules:
  0.0 424.8 jit_solution(10991581283528540992)
XLA Ops:
  6.5 0.7 fusion.42
  7.2 1.2 reduce-window.6
  8.4 0.2 slice_reduce_fusion
  8.7 0.9 fusion.41
  9.7 0.9 multiply_add_fusion
  10.6 1.8 fusion.24
  12.4 25.6 %all_to_all.10 = bf16[32,2,16,512]{3,2,1,0:T(8,128)(2,1)S(1)} all-to-all(bf16[32,2,16,512]{3,2,1,0:T(8,128)(2,1)S(1)} %bitcast.50), channel_id=1, replica_groups=mesh['expert'=32,'tensor'=8] {'expert'}, dimensions={0} | all-to-all | bytes 2097152 | tf_op jit(solution)/shard_map/all_to_all | solution.py:20
  37.9 4.3 %convert_bitcast_fusion = bf16[32,2,16,2048]{3,2,0,1:T(8,128)(2,1)} fusion(bf16[2,512,2048]{2,1,0:T(8,128)(2,1)S(1)} %copy-done.1, bf16[32,2,16,512]{3,2,1,0:T(8,128)(2,1)S(1)} %all_to_all.10), kind=kOutput, calls=%fused_computation.15 | convolution fusion | flops 2149580800 | bytes 9437184 | tf_op jit(solution)/shard_map/sjcd,jdh->sjch/dot_general | solution.py:38
  42.2 0.0 all-reduce.2.cloned.1.call-update
  42.3 0.0 all-gather.4.cloned.1.call-start
  42.3 108.1 %all-reduce.2.cloned.1.call-done = bf16[32,2,16,2048]{3,2,0,1:T(8,128)(2,1)} async-done(((bf16[32,2,16,2048]{3,2,0,1:T(8,128)(2,1)}), bf16[32,2,16,2048]{3,2,0,1:T(8,128)(2,1)}) %all-reduce.2.cloned.1.call-update) | async-done | bytes 4194320 | tf_op jit(solution)/shard_map/psum | solution.py:41
  150.4 5.8 %fusion.30 = bf16[32,2,16,512]{3,2,0,1:T(8,128)(2,1)S(1)} fusion(bf16[2,2048,512]{2,1,0:T(8,128)(2,1)} %param.12, bf16[32,2,16,2048]{3,2,0,1:T(8,128)(2,1)} %all-reduce.2.cloned.1.call-done), kind=kOutput, calls=%fused_computation.30 | convolution fusion | flops 2154299392 | bytes 9437184 | tf_op jit(solution)/shard_map/sjch,jhd->sjcd/dot_general | solution.py:43
  156.2 0.0 copy-start.2
  156.2 0.0 copy-start.4
  156.2 0.1 copy.16
  156.3 24.6 %all_to_all.11 = bf16[32,2,16,512]{3,2,1,0:T(8,128)(2,1)S(1)} all-to-all(bf16[32,2,16,512]{3,2,1,0:T(8,128)(2,1)S(1)} %copy.16), channel_id=1, replica_groups=mesh['expert'=32,'tensor'=8] {'expert'}, dimensions={0} | all-to-all | bytes 2097152 | tf_op jit(solution)/shard_map/all_to_all | solution.py:20
  180.9 1.6 fusion.35
  182.5 0.0 all-gather.4.cloned.1.call-update
  182.5 0.0 all-gather.6.cloned.1.call-start
  182.6 0.7 all-gather.6.cloned.1.call-update
  183.3 0.0 all-gather.8.cloned.1.call-start
  183.3 0.5 all-gather.8.cloned.1.call-update
  183.8 0.2 reduce-scatter.2.cloned.1.call-start
  184.1 48.4 %all-gather.4.cloned.1.call-done = bf16[512,4096]{1,0:T(8,128)(2,1)} async-done(((bf16[512,512]{1,0:T(8,128)(2,1)}), bf16[512,4096]{1,0:T(8,128)(2,1)}) %all-gather.4.cloned.1.call-update) | async-done | bytes 4194320 | tf_op jit(solution)/shard_map/all_gather | solution.py:51
  232.4 3.1 fusion
  235.5 56.4 %all-gather.6.cloned.1.call-done = bf16[4096,1024]{1,0:T(8,128)(2,1)} async-done(((bf16[128,1024]{1,0:T(8,128)(2,1)}), bf16[4096,1024]{1,0:T(8,128)(2,1)}) %all-gather.6.cloned.1.call-update) | async-done | bytes 8388624 | tf_op jit(solution)/shard_map/all_gather | solution.py:25
  292.0 9.6 %fusion.21 = bf16[512,1024]{1,0:T(8,128)(2,1)S(1)} fusion(bf16[4096,1024]{1,0:T(8,128)(2,1)} %all-gather.6.cloned.1.call-done, bf16[512,4096]{1,0:T(8,128)(2,1)} %all-gather.4.cloned.1.call-done, f32[4096]{0:T(1024)S(1)} %copy-done.3, f32[512]{0:T(512)S(1)} %add_rsqrt_fusion), kind=kOutput, calls=%fused_computation.24 | convolution fusion | flops 4308074496 | bytes 13649920 | tf_op jit(solution)/shard_map/dot_general | solution.py:57
  301.6 50.4 %all-gather.8.cloned.1.call-done = bf16[4096,1024]{1,0:T(8,128)(2,1)} async-done(((bf16[128,1024]{1,0:T(8,128)(2,1)}), bf16[4096,1024]{1,0:T(8,128)(2,1)}) %all-gather.8.cloned.1.call-update) | async-done | bytes 8388624 | tf_op jit(solution)/shard_map/all_gather | solution.py:25
  352.0 9.5 %convolution_convert_fusion = bf16[512,4096]{1,0:T(8,128)(2,1)} fusion(bf16[512,1024]{1,0:T(8,128)(2,1)S(1)} %fusion.21, bf16[4096,1024]{1,0:T(8,128)(2,1)} %all-gather.8.cloned.1.call-done), kind=kOutput, calls=%fused_computation.6 | convolution fusion | flops 4297064448 | bytes 13631488 | tf_op jit(solution)/shard_map/dot_general | solution.py:65
  361.5 0.0 reduce-scatter.2.cloned.1.call-update
  361.5 54.7 %reduce-scatter.2.cloned.1.call-done = bf16[512,512]{1,0:T(8,128)(2,1)} async-done(((bf16[512,4096]{1,0:T(8,128)(2,1)}), bf16[512,512]{1,0:T(8,128)(2,1)}) %reduce-scatter.2.cloned.1.call-update) | async-done | bytes 524304 | tf_op jit(solution)/shard_map/reduce_scatter | solution.py:73
  416.3 2.0 add_convert_fusion
  (12 shorter events, 0.1 us)
Async XLA Ops:
  6.5 143.8 %all-reduce.2.cloned.1.call-start = ((), (), s32[]{:S(2)}) async-start(), calls=%async_computation.3 | async-start | bytes 8388608 | tf_op jit(solution)/shard_map/psum | solution.py:41
  8.7 29.2 %copy-start.1 = (bf16[2,512,2048]{2,1,0:T(8,128)(2,1)S(1)}, bf16[2,512,2048]{2,1,0:T(8,128)(2,1)}, u32[]{:S(2)}) copy-start(bf16[2,512,2048]{2,1,0:T(8,128)(2,1)} %param.11) | copy-start | bytes 12582916
  42.3 190.2 %all-gather.4.cloned.1.call-start = ((), (), s32[]{:S(2)}) async-start(), calls=%async_computation.4 | async-start | bytes 4718592 | tf_op jit(solution)/shard_map/all_gather | solution.py:51
  156.2 24.7 %copy-start.2 = (bf16[512,512]{1,0:T(8,128)(2,1)S(1)}, bf16[512,512]{1,0:T(8,128)(2,1)}, u32[]{:S(2)}) copy-start(bf16[512,512]{1,0:T(8,128)(2,1)} %param.8) | copy-start | bytes 1572868
  156.2 24.7 %copy-start.4 = (f32[512,1]{0,1:T(1,128)S(1)}, f32[512,1]{0,1:T(1,128)}, u32[]{:S(2)}) copy-start(f32[512,1]{0,1:T(1,128)} %param.10) | copy-start | bytes 6148
  180.9 111.0 %copy-start.3 = (f32[4096]{0:T(1024)S(1)}, f32[4096]{0:T(1024)}, u32[]{:S(2)}) copy-start(f32[4096]{0:T(1024)} %param.13) | copy-start | bytes 49156
  182.5 109.4 %all-gather.6.cloned.1.call-start = ((), (), s32[]{:S(2)}) async-start(), calls=%async_computation.5 | async-start | bytes 8650752 | tf_op jit(solution)/shard_map/all_gather | solution.py:25
  183.3 168.7 %all-gather.8.cloned.1.call-start = ((), (), s32[]{:S(2)}) async-start(), calls=%async_computation.6 | async-start | bytes 8650752 | tf_op jit(solution)/shard_map/all_gather | solution.py:25
  183.8 232.4 %reduce-scatter.2.cloned.1.call-start = ((), (), s32[]{:S(2)}) async-start(), calls=%async_computation.7 | async-start | bytes 4718592 | tf_op jit(solution)/shard_map/reduce_scatter | solution.py:73
  361.5 54.8 %copy-start = (bf16[512,512]{1,0:T(8,128)(2,1)S(1)}, bf16[512,512]{1,0:T(8,128)(2,1)}, u32[]{:S(2)}) copy-start(bf16[512,512]{1,0:T(8,128)(2,1)} %fusion.35) | copy-start | bytes 1572868
Sparse Core Ops, SparseCore 0:
  42.4 107.9 all-reduce.1
  182.6 49.7 all-gather.3
  235.0 56.9 all-gather.5
  294.4 57.5 all-gather.7
  361.6 54.5 reduce-scatter.1
where the time goes:
time: 425 us
  waiting for transfers between devices  319 us (75%)
  blocking collectives  50.2 us (12%)
  matrix products  32.6 us (8%)
  between operations  13.2 us (3%)
  other arithmetic  8.86 us (2%)
    psum x1, waiting for transfers between devices, shards(): lax.psum(partial_value.astype(jnp.bfloat16), 'tensor').astype(jnp.float32)  108 us
    all_gather x2, waiting for transfers between devices, gather_rows(): lax.all_gather(weight, 'expert', axis=0, tiled=True)  107 us
    reduce_scatter x1, waiting for transfers between devices, shards(): lax.psum_scatter(outputs.astype(jnp.bfloat16), 'tensor', scatter_dimensio...  54.7 us
    all_to_all x2, blocking collectives, trade(): lax.all_to_all(buffer, 'expert', split_axis=0, concat_axis=0, tiled=True)  50.2 us
    all_gather x1, waiting for transfers between devices, shards(): whole = lax.all_gather(mixed, 'tensor', axis=1, tiled=True)  48.4 us
    dot_general x1, matrix products, add_up(): return jnp.dot(normed, piece, preferred_element_type=jnp.float32)  9.58 us
    dot_general x1, matrix products, add_down(): lax.dot_general(ffn_active, piece, (((1,), (1,)), ((), ())), preferred_el...  9.54 us
  transfers between devices with their start and end apart: 5, of which 5 were waited for; matrix products, arithmetic and copies ran while one was open for 3% of the time, Pallas kernels for 0%

commit v1 on v0

--- a/solution.py
+++ b/solution.py
@@ -4,6 +4,21 @@
 from jax.sharding import PartitionSpec as P
 
 EXP_DEV = 2
+
+
+def state_widths(link_axis, sample):
+    n_dev_all = lax.axis_size(link_axis)
+    grid = tuple(((p, (p + 1) % n_dev_all) for p in range(n_dev_all)))
+
+    def balance_zone_over_axis(new):
+        if len(new) == n_dev_all:
+            return new
+        wide_out = balance_zone_over_axis([lax.ppermute(new[0], link_axis, perm=grid), *new])
+        return wide_out
+
+    raw_out = jnp.concatenate(balance_zone_over_axis([sample]), axis=1)
+    moved = jnp.roll(raw_out, (lax.axis_index(link_axis) + 1) * sample.shape[1], 1)
+    return moved
 
 
 def slot_table(expert_col, experts, capacity):
@@ -48,7 +63,7 @@
         selector, returned, (((0,), (0,)), ((), ())), preferred_element_type=jnp.float32
     )
     mixed = (tokens.astype(jnp.float32) + gates * routed).astype(jnp.bfloat16)
-    whole = lax.all_gather(mixed, "tensor", axis=1, tiled=True)
+    whole = state_widths("tensor", sample=mixed)
     whole_f32 = whole.astype(jnp.float32)
     mean_square = jnp.mean(whole_f32 * whole_f32, axis=1, keepdims=True)
     normed = (whole_f32 * lax.rsqrt(mean_square + 1e-06) * norm_gain).astype(jnp.bfloat16)

time: 425 us -> 368 us (0.87)
  waiting for transfers between devices: 319 us -> 269 us
  blocking collectives: 50.2 us -> 25.6 us
  local copies, waits for them, and re-layouts: 0.33 us -> 10.5 us
  starting transfers between devices: 0.34 us -> 7.78 us
    all_gather x2, waiting for transfers between devices: 107 us -> 0.05 us  [gather_rows(): lax.all_gather(weight, 'expert', axis=0, tiled=True)]
    ppermute x0 -> x7, waiting for transfers between devices: none -> 83.5 us  [balance_zone_over_axis(): lax.ppermute(new[0], link_axis, perm=grid)]
    all_gather x1 -> x0, waiting for transfers between devices: 48.4 us -> none  [shards(): whole = lax.all_gather(mixed, 'tensor', axis=1, tiled=True)]
    all_to_all x2 -> x1, blocking collectives: 50.2 us -> 25.6 us  [trade(): lax.all_to_all(buffer, 'expert', split_axis=0, concat_axis=0, tiled=True)]
    all_to_all x0 -> x1, waiting for transfers between devices: none -> 16.9 us  [trade(): lax.all_to_all(buffer, 'expert', split_axis=0, concat_axis=0, tiled=True)]
    unnamed x10 -> x24, local copies, waits for them, and re-layouts: 0.02 us -> 8.15 us
    all_to_all x0 -> x1, starting transfers between devices: none -> 7.55 us  [trade(): lax.all_to_all(buffer, 'expert', split_axis=0, concat_axis=0, tiled=True)]
    reduce_scatter x1, waiting for transfers between devices: 54.7 us -> 60.2 us  [shards(): lax.psum_scatter(outputs.astype(jnp.bfloat16), 'tensor', scatter_dimensio...]
  transfers between devices with their start and end apart: 5 -> 12, of which waited for: 5 -> 10; matrix products, arithmetic and copies ran while one was open for 3% -> 6% of each run, Pallas kernels for 0% -> 0%
where the time goes in v1:
time: 368 us
  waiting for transfers between devices  269 us (73%)
  matrix products  34.4 us (9%)
  blocking collectives  25.6 us (7%)
  between operations  15.1 us (4%)
  local copies, waits for them, and re-layouts  10.5 us (3%)
  starting transfers between devices  7.78 us (2%)
  other arithmetic  5.55 us (2%)
    psum x1, waiting for transfers between devices, shards(): lax.psum(partial_value.astype(jnp.bfloat16), 'tensor').astype(jnp.float32)  107 us
    ppermute x7, waiting for transfers between devices, balance_zone_over_axis(): lax.ppermute(new[0], link_axis, perm=grid)  83.5 us
    reduce_scatter x1, waiting for transfers between devices, shards(): lax.psum_scatter(outputs.astype(jnp.bfloat16), 'tensor', scatter_dimensio...  60.2 us
    all_to_all x1, blocking collectives, trade(): lax.all_to_all(buffer, 'expert', split_axis=0, concat_axis=0, tiled=True)  25.6 us
    all_to_all x1, waiting for transfers between devices, trade(): lax.all_to_all(buffer, 'expert', split_axis=0, concat_axis=0, tiled=True)  16.9 us
    dot_general x1, matrix products, add_up(): return jnp.dot(normed, piece, preferred_element_type=jnp.float32)  9.65 us
    dot_general x1, matrix products, add_down(): lax.dot_general(ffn_active, piece, (((1,), (1,)), ((), ())), preferred_el...  9.54 us
    unnamed x24, local copies, waits for them, and re-layouts  8.15 us
  transfers between devices with their start and end apart: 12, of which 10 were waited for; matrix products, arithmetic and copies ran while one was open for 6% of the time, Pallas kernels for 0%

profile of v1, /device:TPU:1, one launch (start us, length us, event | category | flops | bytes accessed | tf_op | source)
XLA Modules:
  0.0 367.6 jit_solution(741552275235842413)
XLA Ops:
  7.4 0.7 fusion.43
  8.1 1.2 reduce-window.6
  9.5 0.8 fusion.42
  10.3 0.7 multiply_add_fusion
  11.0 1.8 fusion.27
  12.8 25.6 %all_to_all.10 = bf16[32,2,16,512]{3,2,1,0:T(8,128)(2,1)S(1)} all-to-all(bf16[32,2,16,512]{3,2,1,0:T(8,128)(2,1)S(1)} %bitcast.50), channel_id=1, replica_groups=mesh['expert'=32,'tensor'=8] {'expert'}, dimensions={0} | all-to-all | bytes 2097152 | tf_op jit(solution)/shard_map/all_to_all | solution.py:35
  38.4 6.6 %convert_bitcast_fusion = bf16[32,2,16,2048]{3,2,0,1:T(8,128)(2,1)} fusion(bf16[2,512,2048]{2,1,0:T(8,128)(2,1)} %param.11, bf16[32,2,16,512]{3,2,1,0:T(8,128)(2,1)S(1)} %all_to_all.10), kind=kOutput, calls=%fused_computation.15 | convolution fusion | flops 2149580800 | bytes 9437184 | tf_op jit(solution)/shard_map/sjcd,jdh->sjch/dot_general | solution.py:53
  45.6 0.5 all-gather.5.cloned.1.call-update
  46.1 106.9 %all-reduce.2.cloned.1.call-done = bf16[32,2,16,2048]{3,2,0,1:T(8,128)(2,1)} async-done(((bf16[32,2,16,2048]{3,2,0,1:T(8,128)(2,1)}), bf16[32,2,16,2048]{3,2,0,1:T(8,128)(2,1)}) %all-reduce.2.cloned.1.call-update) | async-done | bytes 4194320 | tf_op jit(solution)/shard_map/psum | solution.py:56
  153.1 6.1 %fusion.31 = bf16[32,2,16,512]{3,2,0,1:T(8,128)(2,1)S(1)} fusion(bf16[2,2048,512]{2,1,0:T(8,128)(2,1)} %param.12, bf16[32,2,16,2048]{3,2,0,1:T(8,128)(2,1)} %all-reduce.2.cloned.1.call-done), kind=kOutput, calls=%fused_computation.31 | convolution fusion | flops 2154299392 | bytes 9437184 | tf_op jit(solution)/shard_map/sjch,jhd->sjcd/dot_general | solution.py:58
  159.2 1.0 copy.26
  160.2 7.6 %all-to-all-start.1 = ((bf16[32,2,16,512]{3,2,1,0:T(8,128)(2,1)}), bf16[32,2,16,512]{3,2,1,0:T(8,128)(2,1)S(1)}, u32[]{:S(2)}, u32[]{:S(2)}) async-start(bf16[32,2,16,512]{3,2,1,0:T(8,128)(2,1)} %copy.26), calls=%async_computation.1 | async-start | bytes 2097152 | tf_op jit(solution)/shard_map/all_to_all | solution.py:35
  168.1 16.9 %all-to-all-done.1 = bf16[32,2,16,512]{3,2,1,0:T(8,128)(2,1)S(1)} async-done(((bf16[32,2,16,512]{3,2,1,0:T(8,128)(2,1)}), bf16[32,2,16,512]{3,2,1,0:T(8,128)(2,1)S(1)}, u32[]{:S(2)}, u32[]{:S(2)}) %all-to-all-start.1) | async-done | bytes 1048608 | tf_op jit(solution)/shard_map/all_to_all | solution.py:35
  185.0 0.8 fusion.36
  185.8 14.3 %collective-permute-done = bf16[512,512]{0,1:T(8,128)(2,1)S(1)} collective-permute-done((bf16[512,512]{0,1:T(8,128)(2,1)S(1)}, bf16[512,512]{0,1:T(8,128)(2,1)S(1)}, u32[]{:S(2)}, u32[]{:S(2)}) %collective-permute-start) | collective-permute-done | bytes 524320 | tf_op jit(solution)/shard_map/ppermute | solution.py:16
  200.2 13.4 %collective-permute-done.1 = bf16[512,512]{0,1:T(8,128)(2,1)S(1)} collective-permute-done((bf16[512,512]{0,1:T(8,128)(2,1)S(1)}, bf16[512,512]{0,1:T(8,128)(2,1)S(1)}, u32[]{:S(2)}, u32[]{:S(2)}) %collective-permute-start.1) | collective-permute-done | bytes 524320 | tf_op jit(solution)/shard_map/ppermute | solution.py:16
  213.6 12.5 %collective-permute-done.2 = bf16[512,512]{0,1:T(8,128)(2,1)S(1)} collective-permute-done((bf16[512,512]{0,1:T(8,128)(2,1)S(1)}, bf16[512,512]{0,1:T(8,128)(2,1)S(1)}, u32[]{:S(2)}, u32[]{:S(2)}) %collective-permute-start.2) | collective-permute-done | bytes 524320 | tf_op jit(solution)/shard_map/ppermute | solution.py:16
  226.0 11.6 %collective-permute-done.3 = bf16[512,512]{0,1:T(8,128)(2,1)S(1)} collective-permute-done((bf16[512,512]{0,1:T(8,128)(2,1)S(1)}, bf16[512,512]{0,1:T(8,128)(2,1)S(1)}, u32[]{:S(2)}, u32[]{:S(2)}) %collective-permute-start.3) | collective-permute-done | bytes 524320 | tf_op jit(solution)/shard_map/ppermute | solution.py:16
  237.6 10.6 %collective-permute-done.4 = bf16[512,512]{0,1:T(8,128)(2,1)S(1)} collective-permute-done((bf16[512,512]{0,1:T(8,128)(2,1)S(1)}, bf16[512,512]{0,1:T(8,128)(2,1)S(1)}, u32[]{:S(2)}, u32[]{:S(2)}) %collective-permute-start.4) | collective-permute-done | bytes 524320 | tf_op jit(solution)/shard_map/ppermute | solution.py:16
  248.2 10.5 %collective-permute-done.5 = bf16[512,512]{0,1:T(8,128)(2,1)} collective-permute-done((bf16[512,512]{0,1:T(8,128)(2,1)S(1)}, bf16[512,512]{0,1:T(8,128)(2,1)}, u32[]{:S(2)}, u32[]{:S(2)}) %collective-permute-start.5) | collective-permute-done | bytes 524320 | tf_op jit(solution)/shard_map/ppermute | solution.py:16
  258.7 10.7 %collective-permute-done.6 = bf16[512,512]{0,1:T(8,128)(2,1)} collective-permute-done((bf16[512,512]{0,1:T(8,128)(2,1)}, bf16[512,512]{0,1:T(8,128)(2,1)}, u32[]{:S(2)}, u32[]{:S(2)}) %collective-permute-start.6) | collective-permute-done | bytes 524320 | tf_op jit(solution)/shard_map/ppermute | solution.py:16
  269.4 1.1 constant_dynamic-update-slice_fusion.15
  270.5 1.1 constant_dynamic-update-slice_fusion.14
  271.8 1.1 constant_dynamic-update-slice_fusion.7
  272.9 1.1 constant_dynamic-update-slice_fusion.6
  274.3 3.2 copy-done
  277.5 0.9 fusion
  278.5 9.6 %fusion.22 = bf16[512,1024]{1,0:T(8,128)(2,1)S(1)} fusion(bf16[4096,1024]{1,0:T(8,128)(2,1)} %all-gather.3.cloned.1.call-done, f32[4096]{0:T(1024)S(1)} %copy-done.2, f32[512]{0:T(512)S(1)} %add_rsqrt_fusion, bf16[512,8192]{0,1:T(8,128)(2,1)} %copy-done, s32[]{:T(128)S(6)} %select_n.14), kind=kOutput, calls=%fused_computation.25 | convolution fusion | flops 4308074496 | bytes 13649924 | tf_op jit(solution)/shard_map/dot_general | solution.py:72
  288.2 9.5 %convolution_convert_fusion = bf16[512,4096]{0,1:T(8,128)(2,1)} fusion(bf16[512,1024]{1,0:T(8,128)(2,1)S(1)} %fusion.22, bf16[4096,1024]{1,0:T(8,128)(2,1)} %all-gather.5.cloned.1.call-done), kind=kOutput, calls=%fused_computation.6 | convolution fusion | flops 4297064448 | bytes 13631488 | tf_op jit(solution)/shard_map/dot_general | solution.py:80
  297.7 60.2 %reduce-scatter.2.cloned.1.call-done = bf16[512,512]{0,1:T(8,128)(2,1)} async-done(((bf16[512,4096]{0,1:T(8,128)(2,1)}), bf16[512,512]{0,1:T(8,128)(2,1)}) %reduce-scatter.2.cloned.1.call-update) | async-done | bytes 524304 | tf_op jit(solution)/shard_map/reduce_scatter | solution.py:88
  358.0 1.2 add_convert_fusion
  359.2 1.0 copy.28
  (40 shorter events, 1.8 us)
Async XLA Ops:
  7.4 145.7 %all-reduce.2.cloned.1.call-start = ((), (), s32[]{:S(2)}) async-start(), calls=%async_computation.3 | async-start | bytes 8388608 | tf_op jit(solution)/shard_map/psum | solution.py:56
  44.9 233.5 %all-gather.3.cloned.1.call-start = ((), (), s32[]{:S(2)}) async-start(), calls=%async_computation.4 | async-start | bytes 8650752 | tf_op jit(solution)/shard_map/all_gather | solution.py:40
  45.5 242.6 %all-gather.5.cloned.1.call-start = ((), (), s32[]{:S(2)}) async-start(), calls=%async_computation.5 | async-start | bytes 8650752 | tf_op jit(solution)/shard_map/all_gather | solution.py:40
  46.1 121.7 %copy-start.1 = (bf16[512,512]{1,0:T(8,128)(2,1)S(1)}, bf16[512,512]{1,0:T(8,128)(2,1)}, u32[]{:S(2)}) copy-start(bf16[512,512]{1,0:T(8,128)(2,1)} %param.8) | copy-start | bytes 1572868
  46.1 138.8 %copy-start.3 = (f32[512,1]{0,1:T(1,128)S(1)}, f32[512,1]{0,1:T(1,128)}, u32[]{:S(2)}) copy-start(f32[512,1]{0,1:T(1,128)} %param.10) | copy-start | bytes 6148
  160.2 24.7 %all-to-all-start.1 = ((bf16[32,2,16,512]{3,2,1,0:T(8,128)(2,1)}), bf16[32,2,16,512]{3,2,1,0:T(8,128)(2,1)S(1)}, u32[]{:S(2)}, u32[]{:S(2)}) async-start(bf16[32,2,16,512]{3,2,1,0:T(8,128)(2,1)} %copy.26), calls=%async_computation.1 | async-start | bytes 2097152 | tf_op jit(solution)/shard_map/all_to_all | solution.py:35
  167.8 190.2 %reduce-scatter.2.cloned.1.call-start = ((), (), s32[]{:S(2)}) async-start(), calls=%async_computation.6 | async-start | bytes 4718592 | tf_op jit(solution)/shard_map/reduce_scatter | solution.py:88
  185.8 14.4 %collective-permute-start = (bf16[512,512]{0,1:T(8,128)(2,1)S(1)}, bf16[512,512]{0,1:T(8,128)(2,1)S(1)}, u32[]{:S(2)}, u32[]{:S(2)}) collective-permute-start(bf16[512,512]{0,1:T(8,128)(2,1)S(1)} %fusion.36), channel_id=1, source_target_pairs={{0,1},{1,2},{2,3},{3,4},{4,5},{5,6},{6,7},{7,0},{8,9},{9,10},{10,1... | collective-permute-start | bytes 1572872 | tf_op jit(solution)/shard_map/ppermute | solution.py:16
  200.2 13.4 %collective-permute-start.1 = (bf16[512,512]{0,1:T(8,128)(2,1)S(1)}, bf16[512,512]{0,1:T(8,128)(2,1)S(1)}, u32[]{:S(2)}, u32[]{:S(2)}) collective-permute-start(bf16[512,512]{0,1:T(8,128)(2,1)S(1)} %collective-permute-done), channel_id=1, source_target_pairs={{0,1},{1,2},{2,3},{3,4},{4,5},{5,6},{6,7},{7,0},{8,9},{9,10},{10,1... | collective-permute-start | bytes 1572872 | tf_op jit(solution)/shard_map/ppermute | solution.py:16
  213.6 12.5 %collective-permute-start.2 = (bf16[512,512]{0,1:T(8,128)(2,1)S(1)}, bf16[512,512]{0,1:T(8,128)(2,1)S(1)}, u32[]{:S(2)}, u32[]{:S(2)}) collective-permute-start(bf16[512,512]{0,1:T(8,128)(2,1)S(1)} %collective-permute-done.1), channel_id=1, source_target_pairs={{0,1},{1,2},{2,3},{3,4},{4,5},{5,6},{6,7},{7,0},{8,9},{9,10},{10,1... | collective-permute-start | bytes 1572872 | tf_op jit(solution)/shard_map/ppermute | solution.py:16
  226.0 11.6 %collective-permute-start.3 = (bf16[512,512]{0,1:T(8,128)(2,1)S(1)}, bf16[512,512]{0,1:T(8,128)(2,1)S(1)}, u32[]{:S(2)}, u32[]{:S(2)}) collective-permute-start(bf16[512,512]{0,1:T(8,128)(2,1)S(1)} %collective-permute-done.2), channel_id=1, source_target_pairs={{0,1},{1,2},{2,3},{3,4},{4,5},{5,6},{6,7},{7,0},{8,9},{9,10},{10,1... | collective-permute-start | bytes 1572872 | tf_op jit(solution)/shard_map/ppermute | solution.py:16
  237.6 10.6 %collective-permute-start.4 = (bf16[512,512]{0,1:T(8,128)(2,1)S(1)}, bf16[512,512]{0,1:T(8,128)(2,1)S(1)}, u32[]{:S(2)}, u32[]{:S(2)}) collective-permute-start(bf16[512,512]{0,1:T(8,128)(2,1)S(1)} %collective-permute-done.3), channel_id=1, source_target_pairs={{0,1},{1,2},{2,3},{3,4},{4,5},{5,6},{6,7},{7,0},{8,9},{9,10},{10,1... | collective-permute-start | bytes 1572872 | tf_op jit(solution)/shard_map/ppermute | solution.py:16
  248.2 10.5 %collective-permute-start.5 = (bf16[512,512]{0,1:T(8,128)(2,1)S(1)}, bf16[512,512]{0,1:T(8,128)(2,1)}, u32[]{:S(2)}, u32[]{:S(2)}) collective-permute-start(bf16[512,512]{0,1:T(8,128)(2,1)S(1)} %collective-permute-done.4), channel_id=1, source_target_pairs={{0,1},{1,2},{2,3},{3,4},{4,5},{5,6},{6,7},{7,0},{8,9},{9,10},{10,1... | collective-permute-start | bytes 1572872 | tf_op jit(solution)/shard_map/ppermute | solution.py:16
  258.7 10.7 %collective-permute-start.6 = (bf16[512,512]{0,1:T(8,128)(2,1)}, bf16[512,512]{0,1:T(8,128)(2,1)}, u32[]{:S(2)}, u32[]{:S(2)}) collective-permute-start(bf16[512,512]{0,1:T(8,128)(2,1)} %collective-permute-done.5), channel_id=1, source_target_pairs={{0,1},{1,2},{2,3},{3,4},{4,5},{5,6},{6,7},{7,0},{8,9},{9,10},{10,1... | collective-permute-start | bytes 1572872 | tf_op jit(solution)/shard_map/ppermute | solution.py:16
  271.7 6.8 %copy-start.2 = (f32[4096]{0:T(1024)S(1)}, f32[4096]{0:T(1024)}, u32[]{:S(2)}) copy-start(f32[4096]{0:T(1024)} %param.13) | copy-start | bytes 49156
  274.3 3.2 copy-start
Sparse Core Ops, SparseCore 0:
  45.1 107.9 all-reduce.1
  297.8 60.0 reduce-scatter.1
Sparse Core Ops, SparseCore 1:
  48.0 57.1 all-gather.2
  107.6 57.4 all-gather.4
